TPU v7x, 256 devices: a whole 4x4x8 slice. The times are simulated.
256 devices in a mesh: member: 32 (over y, z_hi, core), space: 8 (over z_lo, x).
Axes of the slice: x: 4, y: 4, z: 8 (z_hi: 4, z_lo: 2; z = z_hi * 2 + z_lo), core: 2. Of those that a mesh axis runs over, the one named last changes fastest.
Arguments:
- state: float32 [256, 256, 3, 512], P('member', 'space'), may hold values from -6 to 6
- depth: float32 [256, 512], P('space'), may hold values from 0.5 to 2
- obs_cell: int32 [8, 32, 32], P('space', 'member'), may hold values from 0 to 511
- obs_value: float32 [8, 32, 32], P('space', 'member'), may hold values from -6 to 6
- obs_var: float32 [8, 32, 32], P('space', 'member'), may hold values from 0.05 to 5
Outputs:
- analysis: float32 [256, 256, 3, 512], P('member', 'space')
Inputs may be any that keep to these rules, and one draw needn't show every extreme that they name: obs_cell[b, t, j] names a cell of the 1 row of tile t of band b, counted row by row.
All inputs are finite; a program needn't handle non-finite values.
Results may differ from a plain program's by a relative error of at most 0.00021.
Values sent between devices are 32-bit elements; how exact they have to be, the bound alone decides.
No kernel may reach another device: no remote copies, remote signals or barrier semaphores. Data moves between devices by JAX's collectives and lax.ppermute only.
A program may use at most 128 MiB of HBM per device.

v0:
```python
import functools

import jax
import jax.numpy as jnp
from jax import lax
from jax.experimental import pallas as pl
from jax.experimental.pallas import tpu as pltpu
from jax.sharding import PartitionSpec as P

STEPS = 3
NS_ITERS = 5
COURANT = 0.3
HALO = 2 * STEPS
LANES = 128
ROW_BLOCK = 4
VMEM = 40 * 1024 * 1024
ALL_VMEM = 60 * 1024 * 1024
HIGHEST = lax.Precision.HIGHEST


def dot(a, b, dims=((1,), (0,))):
    return lax.dot_general(a, b, (dims, ((), ())), precision=HIGHEST, preferred_element_type=jnp.float32)


def halves(a):
    high = a.astype(jnp.bfloat16)
    return high, (a - high.astype(jnp.float32)).astype(jnp.bfloat16)


def dot3(a, b, dims=((1,), (0,))):
    def one(x, y):
        return lax.dot_general(x, y, (dims, ((), ())), preferred_element_type=jnp.float32)

    (a_high, a_low), (b_high, b_low) = a, b
    return one(a_high, b_high) + (one(a_high, b_low) + one(a_low, b_high))


def picked(a, picks):
    high, low = halves(a)
    rest = (a - high.astype(jnp.float32) - low.astype(jnp.float32)).astype(jnp.bfloat16)
    parts = [jnp.dot(x, picks, preferred_element_type=jnp.float32) for x in (high, low, rest)]
    return parts[0] + (parts[1] + parts[2])


def cost(flops, bytes_accessed):
    return pl.CostEstimate(flops=flops, bytes_accessed=bytes_accessed, transcendentals=0)


def edges_kernel(state_ref, depth_ref, first_ref, second_ref, top_ref, bottom_ref, depth_top_ref, depth_bottom_ref, sems):
    members, fields, block, cols = top_ref.shape
    rows = depth_ref.shape[0]
    even = lax.axis_index("space") % 2 == 0
    sides = (
        (bottom_ref, depth_bottom_ref, rows - block, True),
        (top_ref, depth_top_ref, 0, False),
    )
    copies = []
    for side, (field_ref, edge_ref, start, _) in enumerate(sides):
        copies.append([
            pltpu.make_async_copy(state_ref.at[m, :, pl.ds(start, block), :], field_ref.at[m], sems.at[side, m])
            for m in range(members)
        ] + [pltpu.make_async_copy(depth_ref.at[pl.ds(start, block), :], edge_ref, sems.at[side, members])])
        for copy in copies[-1]:
            copy.start()

    def write(out_ref, field_ref, edge_ref, last):
        for c in range(cols // LANES):
            lanes = slice(c * LANES, (c + 1) * LANES)
            at = 0
            for k in range(fields):
                count = HALO if k == 2 else HALO - 1
                first = block - count if last else 0
                for m in range(members):
                    out_ref[c, pl.ds(at + m, count, stride=members), :] = field_ref[m, k, first:first + count, lanes]
                at += count * members
            first = block - HALO + 1 if last else 0
            out_ref[c, at:at + HALO - 1, :] = edge_ref[first:first + HALO - 1, lanes]

    for (field_ref, edge_ref, _, last), waits in zip(sides, copies):
        for copy in waits:
            copy.wait()
        for out_ref, here in ((first_ref, even), (second_ref, jnp.logical_not(even))):
            @pl.when(here if last else jnp.logical_not(here))
            def _():
                write(out_ref, field_ref, edge_ref, last)


def edges(state, depth):
    members, fields, rows, cols = state.shape
    block = 8
    shape = jax.ShapeDtypeStruct((cols // LANES, (3 * HALO - 2) * members + 8, LANES), jnp.float32)
    return pl.pallas_call(
        edges_kernel,
        in_specs=[pl.BlockSpec(memory_space=pl.ANY)] * 2,
        out_shape=[shape] * 2,
        scratch_shapes=[
            pltpu.VMEM((members, fields, block, cols), jnp.float32),
            pltpu.VMEM((members, fields, block, cols), jnp.float32),
            pltpu.VMEM((block, cols), jnp.float32),
            pltpu.VMEM((block, cols), jnp.float32),
            pltpu.SemaphoreType.DMA((2, members + 1)),
        ],
        compiler_params=pltpu.CompilerParams(vmem_limit_bytes=ALL_VMEM),
        cost_estimate=cost(0, 2 * state.size),
        name="edges",
    )(state, depth)


def forecast_kernel(bands, state_ref, first_ref, second_ref, depth_ref, height_ref, wind_ref, field_ref, pull_ref, made_ref, sems):
    members, fields, rows, cols = state_ref.shape
    chunks = cols // LANES
    band = lax.axis_index("space")
    lane = lax.broadcasted_iota(jnp.int32, (1, LANES), 1)

    even = band % 2 == 0

    def above(c, first, last):
        return jnp.where(even, second_ref[c, first:last, :], first_ref[c, first:last, :])

    def below(c, first, last):
        return jnp.where(even, first_ref[c, first:last, :], second_ref[c, first:last, :])

    for c in range(chunks):
        lanes = slice(c * LANES, (c + 1) * LANES)
        at = 0
        for k in range(fields):
            count = HALO if k == 2 else HALO - 1
            size = count * members
            field_ref[k, c, (HALO - count) * members:HALO * members, :] = above(c, at, at + size)
            field_ref[k, c, (HALO + rows) * members:(HALO + rows + count) * members, :] = below(c, at, at + size)
            at += size
            for m in range(members):
                field_ref[k, c, pl.ds(HALO * members + m, rows, stride=members), :] = state_ref[m, k, :, lanes]
        pull_above = COURANT * above(c, at, at + HALO - 1)
        pull_here = COURANT * depth_ref[:, lanes]
        pull_below = COURANT * below(c, at, at + HALO - 1)
        for m in range(members):
            pull_ref[c, pl.ds(members + m, HALO - 1, stride=members), :] = pull_above
            pull_ref[c, pl.ds(HALO * members + m, rows, stride=members), :] = pull_here
            pull_ref[c, pl.ds((HALO + rows) * members + m, HALO - 1, stride=members), :] = pull_below

    def cols_diff(parts):
        left = [pltpu.roll(p, 1, 1) for p in parts]
        right = [pltpu.roll(p, LANES - 1, 1) for p in parts]
        return [
            jnp.where(lane == LANES - 1, right[(c + 1) % chunks], right[c]) - jnp.where(lane == 0, left[c - 1], left[c])
            for c in range(chunks)
        ]

    def take(k, first, count):
        return [field_ref[k, c, first * members:(first + count) * members, :] for c in range(chunks)]

    def push_of(first, count):
        if first >= HALO and first + count <= HALO + rows:
            return COURANT
        row = lax.broadcasted_iota(jnp.int32, (count * members, LANES), 0) + (first + band * rows - HALO) * members
        return jnp.where(jnp.logical_and(row >= 0, row < bands * rows * members), COURANT, 0.0)

    def blocks(first, last):
        cuts = sorted({HALO, HALO + rows} | set(range(HALO, HALO + rows, ROW_BLOCK)))
        ends = [first] + [e for e in cuts if first < e < last] + [last]
        return [(lo, hi - lo) for lo, hi in zip(ends[:-1], ends[1:])]

    copies = []
    for step in range(STEPS):
        reach = 2 * (STEPS - 1 - step)
        for first, count in blocks(HALO - reach - 1, HALO + rows + reach + 1):
            height = take(0, first, count)
            slope = cols_diff(take(1, first, count))
            north = take(2, first + 1, count)
            south = take(2, first - 1, count)
            span = slice(first * members, (first + count) * members)
            for c in range(chunks):
                field_ref[0, c, span, :] = height[c] - pull_ref[c, span, :] * (slope[c] + (north[c] - south[c]))
        for first, count in blocks(HALO - reach, HALO + rows + reach):
            slope = cols_diff(take(0, first, count))
            zonal = take(1, first, count)
            meridional = take(2, first, count)
            north = take(0, first + 1, count)
            south = take(0, first - 1, count)
            push = push_of(first, count)
            span = slice(first * members, (first + count) * members)
            for c in range(chunks):
                zonal[c] = zonal[c] - COURANT * slope[c]
                meridional[c] = meridional[c] - push * (north[c] - south[c])
                if step < STEPS - 1:
                    field_ref[1, c, span, :] = zonal[c]
                    field_ref[2, c, span, :] = meridional[c]
            if step == STEPS - 1:
                here = take(0, first, count)
                for k, parts in enumerate((here, zonal, meridional)):
                    for c in range(chunks):
                        for t in range(count):
                            out_ref, start = (height_ref, 0) if k == 0 else (made_ref, (k - 1) * cols)
                            lanes = slice(start + c * LANES, start + (c + 1) * LANES)
                            out_ref[first - HALO + t, :, lanes] = parts[c][t * members:(t + 1) * members]
                leaving = pl.ds(first - HALO, count)
                copies.append(pltpu.make_async_copy(made_ref.at[leaving], wind_ref.at[leaving], sems.at[len(copies)]))
                copies[-1].start()
    for copy in copies:
        copy.wait()


def forecast(state, first, second, depth, bands):
    members, fields, rows, cols = state.shape
    total = rows + 2 * HALO
    return pl.pallas_call(
        functools.partial(forecast_kernel, bands),
        out_shape=[
            jax.ShapeDtypeStruct((rows, members, cols), jnp.float32),
            jax.ShapeDtypeStruct((rows, members, 2 * cols), jnp.float32),
        ],
        scratch_shapes=[
            pltpu.VMEM((fields, cols // LANES, total * members, LANES), jnp.float32),
            pltpu.VMEM((cols // LANES, total * members, LANES), jnp.float32),
            pltpu.VMEM((rows, members, 2 * cols), jnp.float32),
            pltpu.SemaphoreType.DMA((rows // ROW_BLOCK,)),
        ],
        out_specs=[pl.BlockSpec(memory_space=pltpu.VMEM), pl.BlockSpec(memory_space=pl.ANY)],
        compiler_params=pltpu.CompilerParams(vmem_limit_bytes=VMEM),
        cost_estimate=cost(STEPS * 12 * state.size, 8 * state.size),
        name="forecast",
    )(state, first, second, depth)


TAIL = 8


def corners(size):
    i = lax.broadcasted_iota(jnp.int32, (size, size), 0)
    j = lax.broadcasted_iota(jnp.int32, (size, size), 1)
    return i < j, i == j


def gram_kernel(height_ref, got_ref, cell_ref, value_ref, var_ref, keep_ref, send_ref, seen_ref, whole_ref):
    chips, cores, members, cols = height_ref.shape
    count = chips * cores * members
    number, half, share = cell_ref.shape[1], count // 2, keep_ref.shape[0]
    picks = lax.broadcasted_iota(jnp.int32, (cols, number), 0) == cell_ref[...]
    picks = jnp.where(picks, 1.0, 0.0).astype(jnp.bfloat16)
    core = lax.axis_index("member") % cores
    own = height_ref[:, pl.ds(core, 1)].reshape(half, cols)
    seen_ref[:, pl.ds(core, 1)] = picked(own, picks).reshape(chips, 1, members, number)
    seen_ref[:, pl.ds(1 - core, 1)] = picked(got_ref[...].reshape(half, cols), picks).reshape(chips, 1, members, number)
    seen = seen_ref[...].reshape(count, number)
    centre = jnp.sum(seen, axis=0, keepdims=True) / count
    observed = seen - centre
    innovation = value_ref[...] - centre
    weighted = observed / var_ref[...]
    gram = dot(weighted, observed, ((1,), (1,)))
    projection = jnp.sum(weighted * innovation, axis=1, keepdims=True)
    above, diagonal = corners(half)
    last = gram[half:, half:]
    both = jnp.concatenate([jnp.where(jnp.logical_or(above, diagonal), gram[:half, :half], last), gram[:half, half:]], axis=1)
    tails = (
        jnp.sum(jnp.where(corners(count)[1], projection, 0.0), axis=0, keepdims=True),
        jnp.concatenate([jnp.sum(jnp.where(diagonal, last, 0.0), axis=0, keepdims=True), jnp.zeros((1, half), jnp.float32)], axis=1),
    )
    for side, tail in enumerate(tails):
        first, rows = side * share, share - TAIL
        whole_ref[first:first + rows, :] = both[side * rows:(side + 1) * rows]
        whole_ref[first + rows:first + share, :] = jnp.broadcast_to(tail, (TAIL, count))
    keep_ref[...] = whole_ref[pl.ds(pl.multiple_of(core * share, TAIL), share), :]
    send_ref[...] = whole_ref[pl.ds(pl.multiple_of((1 - core) * share, TAIL), share), :]


def gram_of(height, got, cell, value, var):
    chips, cores, members, cols = height.shape
    count = chips * cores * members
    return pl.pallas_call(
        gram_kernel,
        out_shape=[jax.ShapeDtypeStruct((count // 4 + TAIL, count), jnp.float32)] * 2,
        scratch_shapes=[
            pltpu.VMEM((chips, cores, members, cell.shape[1]), jnp.float32),
            pltpu.VMEM((count // 2 + 2 * TAIL, count), jnp.float32),
        ],
        compiler_params=pltpu.CompilerParams(vmem_limit_bytes=VMEM),
        cost_estimate=cost(6 * 2 * count * cols * cell.shape[1], 4 * count * cols),
        name="gram",
    )(height, got, cell, value, var)


def pick_kernel(first, state_ref, out_ref):
    chips, members, width = out_ref.shape
    other = 1 - lax.axis_index("member") % 2
    out_ref[...] = state_ref[:, pl.ds(other, 1), :, first:first + width].reshape(out_ref.shape)


def pick(state, first, last):
    chips, cores, members, _ = state.shape
    shape = jax.ShapeDtypeStruct((chips, members, last - first), jnp.float32)
    return pl.pallas_call(
        functools.partial(pick_kernel, first),
        out_shape=shape,
        compiler_params=pltpu.CompilerParams(vmem_limit_bytes=VMEM),
        cost_estimate=cost(0, 8 * shape.size),
        name="pick",
    )(state)


def transform_kernel(keep_ref, got_ref, weights_ref, packed_ref):
    share, count = keep_ref.shape
    half, rows = count // 2, share - TAIL
    core = lax.axis_index("member") % 2
    packed_ref[pl.ds(pl.multiple_of(core * share, TAIL), share), :] = keep_ref[...]
    packed_ref[pl.ds(pl.multiple_of((1 - core) * share, TAIL), share), :] = got_ref[...]
    both = jnp.concatenate([packed_ref[:rows, :], packed_ref[share:share + rows, :]], axis=0)
    above, diagonal = corners(half)
    corner, side = both[:, :half], both[:, half:]
    upper = jnp.where(above, corner, 0.0)
    lower = jnp.where(jnp.logical_or(above, diagonal), 0.0, corner)
    one = upper + upper.T + jnp.where(diagonal, corner, 0.0)
    two = lower + lower.T + jnp.where(diagonal, packed_ref[share + rows:share + rows + 1, :half], 0.0)
    gram = jnp.concatenate([jnp.concatenate([one, side], axis=1), jnp.concatenate([side.T, two], axis=1)], axis=0)
    projection = jnp.sum(jnp.where(corners(count)[1], packed_ref[rows:rows + 1, :], 0.0), axis=1, keepdims=True)
    i = lax.broadcasted_iota(jnp.int32, (count, count), 0)
    j = lax.broadcasted_iota(jnp.int32, (count, count), 1)
    identity = jnp.where(i == j, 1.0, 0.0)
    system = identity + gram / (count - 1)
    scale = jnp.sqrt(jnp.sum(jnp.sum(system * system, axis=1, keepdims=True), axis=0, keepdims=True))
    current = system / scale
    root_inv = identity
    for step in range(NS_ITERS):
        parts, inv_parts = halves(current), halves(root_inv)
        product = current if step == 0 else dot3(inv_parts, parts)
        factor = 1.5 * identity - 0.5 * product
        factor_parts = halves(factor)
        if step < NS_ITERS - 1:
            current = dot3(parts, factor_parts)
        root_inv = factor if step == 0 else dot3(factor_parts, inv_parts)
    root = root_inv / jnp.sqrt(scale)

    def times(column):
        return jnp.sum(root * jnp.sum(jnp.where(i == j, column, 0.0), axis=0, keepdims=True), axis=1, keepdims=True)

    weights_ref[...] = times(times(projection)) / (count - 1) + root


def transform(keep, got):
    share, count = keep.shape
    return pl.pallas_call(
        transform_kernel,
        out_shape=jax.ShapeDtypeStruct((count, count), jnp.float32),
        scratch_shapes=[pltpu.VMEM((2 * share, count), jnp.float32)],
        compiler_params=pltpu.CompilerParams(vmem_limit_bytes=VMEM),
        cost_estimate=cost(6 * 2 * 14 * count ** 3, 8 * count ** 2),
        name="transform",
    )(keep, got)


def mix_kernel(weights_ref, height_ref, got_height_ref, wind_ref, got_wind_ref, out_ref, order_ref):
    chips, cores, members, cols = height_ref.shape
    half, count = chips * members, chips * cores * members
    core = lax.axis_index("member") % cores
    for q in range(chips):
        for side, other in ((0, core), (1, 1 - core)):
            start = pl.multiple_of((q * cores + other) * members, members)
            order_ref[side * half + q * members:side * half + (q + 1) * members, :] = weights_ref[pl.ds(start, members), :]
    order = halves(order_ref[...])
    for first in range(0, 3 * cols, cols):
        if first == 0:
            own, got = height_ref[:, pl.ds(core, 1)], got_height_ref[...]
        else:
            own, got = wind_ref[:, pl.ds(core, 1), :, first - cols:first], got_wind_ref[:, :, first - cols:first]
        values = jnp.concatenate([own.reshape(half, cols), got.reshape(half, cols)], axis=0)
        centre = jnp.sum(values, axis=0, keepdims=True) / count
        out_ref[:, first:first + cols] = centre + dot3(order, halves(values - centre), ((0,), (0,)))


def mix(weights, height, got_height, wind, got_wind):
    count, cols = weights.shape[0], height.shape[-1]
    return pl.pallas_call(
        mix_kernel,
        out_shape=jax.ShapeDtypeStruct((count, 3 * cols), jnp.float32),
        scratch_shapes=[pltpu.VMEM(weights.shape, jnp.float32)],
        compiler_params=pltpu.CompilerParams(vmem_limit_bytes=VMEM),
        cost_estimate=cost(3 * 2 * count * count * 3 * cols, 4 * count * 6 * cols),
        name="mix",
    )(weights, height, got_height, wind, got_wind)


def unfold_kernel(rows_ref, out_ref, lanes_ref, whole_ref, sems):
    members, fields, rows, cols = whole_ref.shape
    chunks = cols // LANES
    copies = []
    for k in range(fields):
        for c in range(k * chunks, (k + 1) * chunks):
            lanes_ref[c] = rows_ref[:, c * LANES:(c + 1) * LANES]
        for m in range(members):
            for c in range(chunks):
                whole_ref[m, k, :, c * LANES:(c + 1) * LANES] = lanes_ref[k * chunks + c, pl.ds(m, rows, stride=members), :]
        copies.append(pltpu.make_async_copy(whole_ref.at[:, k], out_ref.at[:, k], sems.at[k]))
        copies[-1].start()
    for copy in copies:
        copy.wait()


def unfold(rows, shape):
    return pl.pallas_call(
        unfold_kernel,
        out_shape=jax.ShapeDtypeStruct(shape, jnp.float32),
        out_specs=pl.BlockSpec(memory_space=pl.ANY),
        scratch_shapes=[
            pltpu.VMEM((rows.shape[1] // LANES, rows.shape[0], LANES), jnp.float32),
            pltpu.VMEM(shape, jnp.float32),
            pltpu.SemaphoreType.DMA((shape[1],)),
        ],
        compiler_params=pltpu.CompilerParams(vmem_limit_bytes=VMEM),
        cost_estimate=cost(0, 8 * rows.size),
        name="unfold",
    )(rows)


def exchange(blocks, axis, groups=None):
    return lax.all_to_all(blocks, axis, split_axis=0, concat_axis=0, tiled=True, axis_index_groups=groups)


def shards(state, depth, obs_cell, obs_value, obs_var):
    bands, tiles = lax.axis_size("space"), lax.axis_size("member")
    members, rows, fields, cols = state.shape
    ensemble, chips = tiles * members, tiles // 2
    sibling = [(i, i ^ 1) for i in range(tiles)]

    state = state.transpose(0, 2, 1, 3)
    upper = [(i, i ^ 1) for i in range(bands)]
    lower = [pair for i in range(1, bands - 1, 2) for pair in ((i, i + 1), (i + 1, i))]

    first, second = edges(state, depth)
    first = lax.ppermute(first, "space", upper)
    second = lax.ppermute(second, "space", lower)
    height, wind = forecast(state, first, second, depth, bands)
    same_core = [[2 * q + core for q in range(chips)] for core in range(2)]

    def to_sibling(values):
        return lax.ppermute(pick(values, 0, values.shape[-1]), "member", sibling)

    height = exchange(height.reshape(chips, 2, members, cols), "member", same_core)
    height, wind = lax.optimization_barrier((height, wind))
    wind = exchange(wind.reshape(chips, 2, members, 2 * cols), "member", same_core)
    got_height = to_sibling(height)

    keep, send = gram_of(height, got_height, obs_cell[0], obs_value[0], obs_var[0])
    half = keep + lax.ppermute(send, "member", sibling)

    def others(value, axis, unit):
        return [lax.ppermute(value, axis, [(i, i ^ (unit * k)) for i in range(lax.axis_size(axis))]) for k in (1, 2, 3)]

    for axis, unit in (("space", 1), ("member", tiles // 4)):
        one, two, three = others(half, axis, unit)
        half = (half + one) + (two + three)
    one, two, three = others(half, "member", 2)
    half = (half + one) + (two + three)
    half, wind = lax.optimization_barrier((half, wind))
    beside = [(m * bands + i, (m ^ 1) * bands + (i ^ 4)) for m in range(tiles) for i in range(bands)]
    near = lax.ppermute(half, "space", [(i, i ^ 4) for i in range(bands)])
    far = lax.ppermute(half, ("member", "space"), beside)
    weights = transform(half + near, lax.ppermute(half, "member", sibling) + far)

    analysed = mix(weights, height, got_height, wind, to_sibling(wind))
    back = exchange(analysed.reshape(tiles, members, fields * cols), "member").reshape(ensemble, fields * cols)
    return unfold(back, (members, fields, rows, cols)).transpose(0, 2, 1, 3)


def solution(mesh):
    placed = (
        P("member", "space", None, None),
        P("space", None),
        P("space", "member", None),
        P("space", "member", None),
        P("space", "member", None),
    )
    return jax.shard_map(
        shards,
        mesh=mesh,
        in_specs=placed,
        out_specs=P("member", "space", None, None),
        check_vma=False,
    )
```

profile of v0, /device:TPU:1, one launch (start us, length us, event | category | flops | bytes accessed | tf_op | source)
XLA Modules:
  0.0 147.0 jit_solution(12145257148164345040)
XLA Ops:
  0.0 2.3 %edges.1 = (f32[4,136,128]{2,1,0:T(8,128)}, f32[4,136,128]{2,1,0:T(8,128)}) custom-call(f32[8,3,32,512]{3,2,1,0:T(8,128)} %bitcast.9, f32[32,512]{1,0:T(8,128)} %depth_ref.3), custom_call_target="tpu_custom_call" | custom-call | bytes 786432 | tf_op jit(solution)/shard_map/edges/pallas_call | solution.py:92
  2.3 2.1 %collective-permute-start = (f32[4,136,128]{2,1,0:T(8,128)}, f32[4,136,128]{2,1,0:T(8,128)S(1)}, u32[]{:S(2)}, u32[]{:S(2)}) collective-permute-start(f32[4,136,128]{2,1,0:T(8,128)} %get-tuple-element.15), channel_id=1, source_target_pairs={{0,1},{1,0},{2,3},{3,2},{4,5},{5,4},{6,7},{7,6},{8,9},{9,8},{10,11... | collective-permute-start | bytes 835592 | tf_op jit(solution)/shard_map/ppermute | solution.py:429
  4.4 0.7 collective-permute-start.1
  5.1 4.7 %collective-permute-done.first_ref = f32[4,136,128]{2,1,0:T(8,128)S(1)} collective-permute-done((f32[4,136,128]{2,1,0:T(8,128)}, f32[4,136,128]{2,1,0:T(8,128)S(1)}, u32[]{:S(2)}, u32[]{:S(2)}) %collective-permute-start) | collective-permute-done | bytes 278560 | tf_op jit(solution)/shard_map/ppermute | solution.py:429
  9.8 3.0 %forecast.1 = (f32[32,8,512]{2,1,0:T(8,128)S(1)}, f32[32,8,1024]{2,1,0:T(8,128)}) custom-call(f32[8,3,32,512]{3,2,1,0:T(8,128)S(1)} %bitcast.10, f32[4,136,128]{2,1,0:T(8,128)S(1)} %collective-permute-done.first_ref, f32[4,136,128]{2,1,0:T(8,128)S(1)} %collective-permute-done.1.second_ref, f32[32,512]{1,0:T(8,128)S(1)} %copy-done.1), custom_call_target="tpu_custom_call" | custom-call | flops 14155776 | bytes 3145728 | tf_op jit(solution)/shard_map/forecast/pallas_call | solution.py:207
  12.8 27.3 %all_to_all.15.state_ref.height_ref = f32[16,2,8,512]{3,2,1,0:T(8,128)S(1)} all-to-all(f32[16,2,8,512]{3,2,1,0:T(8,128)S(1)} %bitcast.13), channel_id=1, replica_groups={{0,16,32,48,64,80,96,112,128,144,160,176,192,208,224,240},{8,24,40,56,7..., dimensions={0} | all-to-all | bytes 1048576 | tf_op jit(solution)/shard_map/all_to_all | solution.py:415
  40.1 3.8 %all-to-all-start.1 = ((f32[16,2,8,1024]{3,2,1,0:T(8,128)}), f32[16,2,8,1024]{3,2,1,0:T(8,128)S(1)}, u32[]{:S(2)}, u32[]{:S(2)}) async-start(f32[16,2,8,1024]{3,2,1,0:T(8,128)} %bitcast.5), calls=%async_computation.1 | async-start | bytes 2097152 | tf_op jit(solution)/shard_map/all_to_all | solution.py:415
  43.9 3.7 %collective-permute-start.2 = (f32[16,8,512]{2,1,0:T(8,128)S(1)}, f32[16,8,512]{2,1,0:T(8,128)S(1)}, u32[]{:S(2)}, u32[]{:S(2)}) collective-permute-start(f32[16,8,512]{2,1,0:T(8,128)S(1)} %pick.2), channel_id=1, source_target_pairs={{0,8},{8,0},{16,24},{24,16},{32,40},{40,32},{48,56},{56,48},{64,72... | collective-permute-start | bytes 786440 | tf_op jit(solution)/shard_map/ppermute | solution.py:435
  47.6 1.2 collective-permute-done.2.got_ref.got_height_ref
  48.8 0.9 gram.1
  49.6 0.5 collective-permute-start.3
  50.1 0.9 collective-permute-done.3
  51.0 5.5 %collective-permute-start.6 = (f32[72,256]{1,0:T(8,128)S(1)}, f32[72,256]{1,0:T(8,128)S(1)}, u32[]{:S(2)}, u32[]{:S(2)}) collective-permute-start(f32[72,256]{1,0:T(8,128)S(1)} %add.36), channel_id=1, source_target_pairs={{0,3},{1,2},{2,1},{3,0},{4,7},{5,6},{6,5},{7,4},{8,11},{9,10},{10,... | collective-permute-start | bytes 221192 | tf_op jit(solution)/shard_map/ppermute | solution.py:446
  56.5 1.0 collective-permute-start.5
  57.5 2.0 %collective-permute-done.6 = f32[72,256]{1,0:T(8,128)S(1)} collective-permute-done((f32[72,256]{1,0:T(8,128)S(1)}, f32[72,256]{1,0:T(8,128)S(1)}, u32[]{:S(2)}, u32[]{:S(2)}) %collective-permute-start.6) | collective-permute-done | bytes 73760 | tf_op jit(solution)/shard_map/ppermute | solution.py:446
  59.5 1.9 %collective-permute-done.5 = f32[72,256]{1,0:T(8,128)S(1)} collective-permute-done((f32[72,256]{1,0:T(8,128)S(1)}, f32[72,256]{1,0:T(8,128)S(1)}, u32[]{:S(2)}, u32[]{:S(2)}) %collective-permute-start.5) | collective-permute-done | bytes 73760 | tf_op jit(solution)/shard_map/ppermute | solution.py:446
  61.5 2.9 %collective-permute-start.9 = (f32[72,256]{1,0:T(8,128)S(1)}, f32[72,256]{1,0:T(8,128)S(1)}, u32[]{:S(2)}, u32[]{:S(2)}) collective-permute-start(f32[72,256]{1,0:T(8,128)S(1)} %add_add_fusion.2), channel_id=1, source_target_pairs={{0,192},{8,200},{16,208},{24,216},{32,224},{40,232},{48,240},{56,2... | collective-permute-start | bytes 221192 | tf_op jit(solution)/shard_map/ppermute | solution.py:446
  64.4 0.4 collective-permute-start.8
  65.1 1.4 collective-permute-done.9
  66.5 3.4 %collective-permute-done.8 = f32[72,256]{1,0:T(8,128)S(1)} collective-permute-done((f32[72,256]{1,0:T(8,128)S(1)}, f32[72,256]{1,0:T(8,128)S(1)}, u32[]{:S(2)}, u32[]{:S(2)}) %collective-permute-start.8) | collective-permute-done | bytes 73760 | tf_op jit(solution)/shard_map/ppermute | solution.py:446
  69.9 2.6 %collective-permute-start.12 = (f32[72,256]{1,0:T(8,128)S(1)}, f32[72,256]{1,0:T(8,128)S(1)}, u32[]{:S(2)}, u32[]{:S(2)}) collective-permute-start(f32[72,256]{1,0:T(8,128)S(1)} %add_add_fusion.1), channel_id=1, source_target_pairs={{0,48},{8,56},{16,32},{24,40},{32,16},{40,24},{48,0},{56,8},{64,11... | collective-permute-start | bytes 221192 | tf_op jit(solution)/shard_map/ppermute | solution.py:446
  72.5 2.1 %collective-permute-start.11 = (f32[72,256]{1,0:T(8,128)S(1)}, f32[72,256]{1,0:T(8,128)S(1)}, u32[]{:S(2)}, u32[]{:S(2)}) collective-permute-start(f32[72,256]{1,0:T(8,128)S(1)} %add_add_fusion.1), channel_id=1, source_target_pairs={{0,32},{8,40},{16,48},{24,56},{32,0},{40,8},{48,16},{56,24},{64,96... | collective-permute-start | bytes 221192 | tf_op jit(solution)/shard_map/ppermute | solution.py:446
  74.6 1.0 collective-permute-start.10
  75.6 4.0 %collective-permute-done.11 = f32[72,256]{1,0:T(8,128)S(1)} collective-permute-done((f32[72,256]{1,0:T(8,128)S(1)}, f32[72,256]{1,0:T(8,128)S(1)}, u32[]{:S(2)}, u32[]{:S(2)}) %collective-permute-start.11) | collective-permute-done | bytes 73760 | tf_op jit(solution)/shard_map/ppermute | solution.py:446
  79.8 7.1 %collective-permute-start.16 = (f32[16,8,1024]{2,1,0:T(8,128)S(1)}, f32[16,8,1024]{2,1,0:T(8,128)S(1)}, u32[]{:S(2)}, u32[]{:S(2)}) collective-permute-start(f32[16,8,1024]{2,1,0:T(8,128)S(1)} %pick.3), channel_id=1, source_target_pairs={{0,8},{8,0},{16,24},{24,16},{32,40},{40,32},{48,56},{56,48},{64,72... | collective-permute-start | bytes 1572872 | tf_op jit(solution)/shard_map/ppermute | solution.py:435
  86.9 1.7 %collective-permute-start.13 = (f32[72,256]{1,0:T(8,128)S(1)}, f32[72,256]{1,0:T(8,128)S(1)}, u32[]{:S(2)}, u32[]{:S(2)}) collective-permute-start(f32[72,256]{1,0:T(8,128)S(1)} %add_add_fusion), channel_id=1, source_target_pairs={{0,4},{1,5},{2,6},{3,7},{4,0},{5,1},{6,2},{7,3},{8,12},{9,13},{10,... | collective-permute-start | bytes 221192 | tf_op jit(solution)/shard_map/ppermute | solution.py:455
  88.9 2.1 %collective-permute-done.13 = f32[72,256]{1,0:T(8,128)S(1)} collective-permute-done((f32[72,256]{1,0:T(8,128)S(1)}, f32[72,256]{1,0:T(8,128)S(1)}, u32[]{:S(2)}, u32[]{:S(2)}) %collective-permute-start.13) | collective-permute-done | bytes 73760 | tf_op jit(solution)/shard_map/ppermute | solution.py:455
  91.1 1.7 %collective-permute-done.15 = f32[72,256]{1,0:T(8,128)S(1)} collective-permute-done((f32[72,256]{1,0:T(8,128)S(1)}, f32[72,256]{1,0:T(8,128)S(1)}, u32[]{:S(2)}, u32[]{:S(2)}) %collective-permute-start.15) | collective-permute-done | bytes 73760 | tf_op jit(solution)/shard_map/ppermute | solution.py:456
  92.8 3.4 %transform.1.weights_ref = f32[256,256]{1,0:T(8,128)S(1)} custom-call(f32[72,256]{1,0:T(8,128)S(1)} %add.46.keep_ref, f32[72,256]{1,0:T(8,128)S(1)} %add.47.got_ref), custom_call_target="tpu_custom_call" | custom-call | flops 2818572288 | bytes 524288 | tf_op jit(solution)/shard_map/transform/pallas_call | solution.py:341
  96.2 0.9 mix.1
  97.1 48.4 %all_to_all.16 = f32[32,8,1536]{2,1,0:T(8,128)S(1)} all-to-all(f32[32,8,1536]{2,1,0:T(8,128)S(1)} %bitcast.12), channel_id=1, replica_groups=mesh['member'=32,'space'=8] {'member'}, dimensions={0} | all-to-all | bytes 3145728 | tf_op jit(solution)/shard_map/all_to_all | solution.py:415
  145.5 1.3 unfold.1
  (30 shorter events, 1.0 us)
Async XLA Ops:
  0.0 9.8 %copy-start.1 = (f32[32,512]{1,0:T(8,128)S(1)}, f32[32,512]{1,0:T(8,128)}, u32[]{:S(2)}) copy-start(f32[32,512]{1,0:T(8,128)} %depth_ref.3) | copy-start | bytes 196612
  0.0 9.8 %copy-start = (f32[8,32,3,512]{3,1,2,0:T(8,128)S(1)}, f32[8,32,3,512]{3,1,2,0:T(8,128)}, u32[]{:S(2)}) copy-start(f32[8,32,3,512]{3,1,2,0:T(8,128)} %param.5) | copy-start | bytes 4718596
  2.3 7.5 %collective-permute-start = (f32[4,136,128]{2,1,0:T(8,128)}, f32[4,136,128]{2,1,0:T(8,128)S(1)}, u32[]{:S(2)}, u32[]{:S(2)}) collective-permute-start(f32[4,136,128]{2,1,0:T(8,128)} %get-tuple-element.15), channel_id=1, source_target_pairs={{0,1},{1,0},{2,3},{3,2},{4,5},{5,4},{6,7},{7,6},{8,9},{9,8},{10,11... | collective-permute-start | bytes 835592 | tf_op jit(solution)/shard_map/ppermute | solution.py:429
  4.4 5.4 %collective-permute-start.1 = (f32[4,136,128]{2,1,0:T(8,128)}, f32[4,136,128]{2,1,0:T(8,128)S(1)}, u32[]{:S(2)}, u32[]{:S(2)}) collective-permute-start(f32[4,136,128]{2,1,0:T(8,128)} %get-tuple-element.16), channel_id=1, source_target_pairs={{1,2},{2,1},{3,4},{4,3},{5,6},{6,5},{9,10},{10,9},{11,12},{12,11},... | collective-permute-start | bytes 835592 | tf_op jit(solution)/shard_map/ppermute | solution.py:430
  40.1 8.7 %copy-start.2 = (s32[1,1,32]{2,1,0:T(1,128)S(1)}, s32[1,1,32]{2,1,0:T(1,128)}, u32[]{:S(2)}) copy-start(s32[1,1,32]{2,1,0:T(1,128)} %param.7) | copy-start | bytes 388
  40.1 8.7 %copy-start.3 = (f32[1,1,32]{2,1,0:T(1,128)S(1)}, f32[1,1,32]{2,1,0:T(1,128)}, u32[]{:S(2)}) copy-start(f32[1,1,32]{2,1,0:T(1,128)} %param.8) | copy-start | bytes 388
  40.1 8.7 %copy-start.4 = (f32[1,1,32]{2,1,0:T(1,128)S(1)}, f32[1,1,32]{2,1,0:T(1,128)}, u32[]{:S(2)}) copy-start(f32[1,1,32]{2,1,0:T(1,128)} %param.9) | copy-start | bytes 388
  40.1 39.6 %all-to-all-start.1 = ((f32[16,2,8,1024]{3,2,1,0:T(8,128)}), f32[16,2,8,1024]{3,2,1,0:T(8,128)S(1)}, u32[]{:S(2)}, u32[]{:S(2)}) async-start(f32[16,2,8,1024]{3,2,1,0:T(8,128)} %bitcast.5), calls=%async_computation.1 | async-start | bytes 2097152 | tf_op jit(solution)/shard_map/all_to_all | solution.py:415
  43.9 4.8 %collective-permute-start.2 = (f32[16,8,512]{2,1,0:T(8,128)S(1)}, f32[16,8,512]{2,1,0:T(8,128)S(1)}, u32[]{:S(2)}, u32[]{:S(2)}) collective-permute-start(f32[16,8,512]{2,1,0:T(8,128)S(1)} %pick.2), channel_id=1, source_target_pairs={{0,8},{8,0},{16,24},{24,16},{32,40},{40,32},{48,56},{56,48},{64,72... | collective-permute-start | bytes 786440 | tf_op jit(solution)/shard_map/ppermute | solution.py:435
  49.6 1.4 collective-permute-start.3
  51.0 8.5 %collective-permute-start.6 = (f32[72,256]{1,0:T(8,128)S(1)}, f32[72,256]{1,0:T(8,128)S(1)}, u32[]{:S(2)}, u32[]{:S(2)}) collective-permute-start(f32[72,256]{1,0:T(8,128)S(1)} %add.36), channel_id=1, source_target_pairs={{0,3},{1,2},{2,1},{3,0},{4,7},{5,6},{6,5},{7,4},{8,11},{9,10},{10,... | collective-permute-start | bytes 221192 | tf_op jit(solution)/shard_map/ppermute | solution.py:446
  56.5 5.0 %collective-permute-start.5 = (f32[72,256]{1,0:T(8,128)S(1)}, f32[72,256]{1,0:T(8,128)S(1)}, u32[]{:S(2)}, u32[]{:S(2)}) collective-permute-start(f32[72,256]{1,0:T(8,128)S(1)} %add.36), channel_id=1, source_target_pairs={{0,2},{1,3},{2,0},{3,1},{4,6},{5,7},{6,4},{7,5},{8,10},{9,11},{10,... | collective-permute-start | bytes 221192 | tf_op jit(solution)/shard_map/ppermute | solution.py:446
  57.5 4.0 %collective-permute-start.4 = (f32[72,256]{1,0:T(8,128)S(1)}, f32[72,256]{1,0:T(8,128)S(1)}, u32[]{:S(2)}, u32[]{:S(2)}) collective-permute-start(f32[72,256]{1,0:T(8,128)S(1)} %add.36), channel_id=1, source_target_pairs={{0,1},{1,0},{2,3},{3,2},{4,5},{5,4},{6,7},{7,6},{8,9},{9,8},{10,11... | collective-permute-start | bytes 221192 | tf_op jit(solution)/shard_map/ppermute | solution.py:446
  61.5 5.0 %collective-permute-start.9 = (f32[72,256]{1,0:T(8,128)S(1)}, f32[72,256]{1,0:T(8,128)S(1)}, u32[]{:S(2)}, u32[]{:S(2)}) collective-permute-start(f32[72,256]{1,0:T(8,128)S(1)} %add_add_fusion.2), channel_id=1, source_target_pairs={{0,192},{8,200},{16,208},{24,216},{32,224},{40,232},{48,240},{56,2... | collective-permute-start | bytes 221192 | tf_op jit(solution)/shard_map/ppermute | solution.py:446
  64.4 5.5 %collective-permute-start.8 = (f32[72,256]{1,0:T(8,128)S(1)}, f32[72,256]{1,0:T(8,128)S(1)}, u32[]{:S(2)}, u32[]{:S(2)}) collective-permute-start(f32[72,256]{1,0:T(8,128)S(1)} %add_add_fusion.2), channel_id=1, source_target_pairs={{0,128},{8,136},{16,144},{24,152},{32,160},{40,168},{48,176},{56,1... | collective-permute-start | bytes 221192 | tf_op jit(solution)/shard_map/ppermute | solution.py:446
  64.8 5.1 %collective-permute-start.7 = (f32[72,256]{1,0:T(8,128)S(1)}, f32[72,256]{1,0:T(8,128)S(1)}, u32[]{:S(2)}, u32[]{:S(2)}) collective-permute-start(f32[72,256]{1,0:T(8,128)S(1)} %add_add_fusion.2), channel_id=1, source_target_pairs={{0,64},{8,72},{16,80},{24,88},{32,96},{40,104},{48,112},{56,120},{... | collective-permute-start | bytes 221192 | tf_op jit(solution)/shard_map/ppermute | solution.py:446
  69.9 5.7 %collective-permute-start.12 = (f32[72,256]{1,0:T(8,128)S(1)}, f32[72,256]{1,0:T(8,128)S(1)}, u32[]{:S(2)}, u32[]{:S(2)}) collective-permute-start(f32[72,256]{1,0:T(8,128)S(1)} %add_add_fusion.1), channel_id=1, source_target_pairs={{0,48},{8,56},{16,32},{24,40},{32,16},{40,24},{48,0},{56,8},{64,11... | collective-permute-start | bytes 221192 | tf_op jit(solution)/shard_map/ppermute | solution.py:446
  72.5 7.2 %collective-permute-start.11 = (f32[72,256]{1,0:T(8,128)S(1)}, f32[72,256]{1,0:T(8,128)S(1)}, u32[]{:S(2)}, u32[]{:S(2)}) collective-permute-start(f32[72,256]{1,0:T(8,128)S(1)} %add_add_fusion.1), channel_id=1, source_target_pairs={{0,32},{8,40},{16,48},{24,56},{32,0},{40,8},{48,16},{56,24},{64,96... | collective-permute-start | bytes 221192 | tf_op jit(solution)/shard_map/ppermute | solution.py:446
  74.6 5.1 %collective-permute-start.10 = (f32[72,256]{1,0:T(8,128)S(1)}, f32[72,256]{1,0:T(8,128)S(1)}, u32[]{:S(2)}, u32[]{:S(2)}) collective-permute-start(f32[72,256]{1,0:T(8,128)S(1)} %add_add_fusion.1), channel_id=1, source_target_pairs={{0,16},{8,24},{16,0},{24,8},{32,48},{40,56},{48,32},{56,40},{64,80... | collective-permute-start | bytes 221192 | tf_op jit(solution)/shard_map/ppermute | solution.py:446
  79.8 16.4 %collective-permute-start.16 = (f32[16,8,1024]{2,1,0:T(8,128)S(1)}, f32[16,8,1024]{2,1,0:T(8,128)S(1)}, u32[]{:S(2)}, u32[]{:S(2)}) collective-permute-start(f32[16,8,1024]{2,1,0:T(8,128)S(1)} %pick.3), channel_id=1, source_target_pairs={{0,8},{8,0},{16,24},{24,16},{32,40},{40,32},{48,56},{56,48},{64,72... | collective-permute-start | bytes 1572872 | tf_op jit(solution)/shard_map/ppermute | solution.py:435
  86.9 4.2 %collective-permute-start.13 = (f32[72,256]{1,0:T(8,128)S(1)}, f32[72,256]{1,0:T(8,128)S(1)}, u32[]{:S(2)}, u32[]{:S(2)}) collective-permute-start(f32[72,256]{1,0:T(8,128)S(1)} %add_add_fusion), channel_id=1, source_target_pairs={{0,4},{1,5},{2,6},{3,7},{4,0},{5,1},{6,2},{7,3},{8,12},{9,13},{10,... | collective-permute-start | bytes 221192 | tf_op jit(solution)/shard_map/ppermute | solution.py:455
  88.5 4.2 %collective-permute-start.15 = (f32[72,256]{1,0:T(8,128)S(1)}, f32[72,256]{1,0:T(8,128)S(1)}, u32[]{:S(2)}, u32[]{:S(2)}) collective-permute-start(f32[72,256]{1,0:T(8,128)S(1)} %add_add_fusion), channel_id=1, source_target_pairs={{0,12},{1,13},{2,14},{3,15},{4,8},{5,9},{6,10},{7,11},{8,4},{9,5},... | collective-permute-start | bytes 221192 | tf_op jit(solution)/shard_map/ppermute | solution.py:456
  88.8 4.0 %collective-permute-start.14 = (f32[72,256]{1,0:T(8,128)S(1)}, f32[72,256]{1,0:T(8,128)S(1)}, u32[]{:S(2)}, u32[]{:S(2)}) collective-permute-start(f32[72,256]{1,0:T(8,128)S(1)} %add_add_fusion), channel_id=1, source_target_pairs={{0,8},{8,0},{16,24},{24,16},{32,40},{40,32},{48,56},{56,48},{64,72... | collective-permute-start | bytes 221192 | tf_op jit(solution)/shard_map/ppermute | solution.py:457
where the time goes:
time: 147 us
  blocking collectives  75.7 us (51%)
  starting transfers between devices  35.7 us (24%)
  waiting for transfers between devices  23.4 us (16%)
  Pallas kernels  11.8 us (8%)
    all_to_all x2, blocking collectives, exchange(): lax.all_to_all(blocks, axis, split_axis=0, concat_axis=0, tiled=True, axi...  75.7 us
    ppermute x9, starting transfers between devices, others(): lax.ppermute(value, axis, [(i, i ^ unit * k) for i in range(lax.axis_size...  15.8 us
    ppermute x9, waiting for transfers between devices, others(): lax.ppermute(value, axis, [(i, i ^ unit * k) for i in range(lax.axis_size...  12.8 us
    ppermute x2, starting transfers between devices, to_sibling(): return lax.ppermute(pick(values, 0, values.shape[-1]), 'member', sibling)  10.8 us
    ppermute x1, waiting for transfers between devices, shards(): first = lax.ppermute(first, 'space', upper)  4.68 us
    all_to_all x1, starting transfers between devices, exchange(): lax.all_to_all(blocks, axis, split_axis=0, concat_axis=0, tiled=True, axi...  3.79 us
    pallas_call x1, Pallas kernels, transform(): pl.pallas_call(transform_kernel, out_shape=jax.ShapeDtypeStruct((count, c...  3.35 us
    pallas_call x1, Pallas kernels, forecast(): pl.pallas_call(functools.partial(forecast_kernel, bands), out_shape=[jax....  3.01 us
  transfers between devices with their start and end apart: 18, of which 10 were waited for; matrix products, arithmetic and copies ran while one was open for 0% of the time, Pallas kernels for 3%

commit v1 on v0

--- a/solution.py
+++ b/solution.py
@@ -348,7 +348,7 @@
     )(keep, got)
 
 
-def mix_kernel(weights_ref, height_ref, got_height_ref, wind_ref, got_wind_ref, out_ref, order_ref):
+def mix_kernel(weights_ref, height_ref, got_height_ref, wind_ref, out_ref, order_ref):
     chips, cores, members, cols = height_ref.shape
     half, count = chips * members, chips * cores * members
     core = lax.axis_index("member") % cores
@@ -356,18 +356,20 @@
         for side, other in ((0, core), (1, 1 - core)):
             start = pl.multiple_of((q * cores + other) * members, members)
             order_ref[side * half + q * members:side * half + (q + 1) * members, :] = weights_ref[pl.ds(start, members), :]
-    order = halves(order_ref[...])
-    for first in range(0, 3 * cols, cols):
-        if first == 0:
-            own, got = height_ref[:, pl.ds(core, 1)], got_height_ref[...]
-        else:
-            own, got = wind_ref[:, pl.ds(core, 1), :, first - cols:first], got_wind_ref[:, :, first - cols:first]
-        values = jnp.concatenate([own.reshape(half, cols), got.reshape(half, cols)], axis=0)
+
+    def mixed(values, coefficients):
         centre = jnp.sum(values, axis=0, keepdims=True) / count
-        out_ref[:, first:first + cols] = centre + dot3(order, halves(values - centre), ((0,), (0,)))
-
-
-def mix(weights, height, got_height, wind, got_wind):
+        return centre + dot3(coefficients, halves(values - centre), ((0,), (0,)))
+
+    own = height_ref[:, pl.ds(core, 1)].reshape(half, cols)
+    heights = jnp.concatenate([own, got_height_ref[...].reshape(half, cols)], axis=0)
+    out_ref[:, :cols] = mixed(heights, halves(order_ref[...]))
+    weights = halves(weights_ref[...])
+    for first in (0, cols):
+        out_ref[:, cols + first:2 * cols + first] = mixed(wind_ref[:, first:first + cols], weights)
+
+
+def mix(weights, height, got_height, wind):
     count, cols = weights.shape[0], height.shape[-1]
     return pl.pallas_call(
         mix_kernel,
@@ -376,7 +378,7 @@
         compiler_params=pltpu.CompilerParams(vmem_limit_bytes=VMEM),
         cost_estimate=cost(3 * 2 * count * count * 3 * cols, 4 * count * 6 * cols),
         name="mix",
-    )(weights, height, got_height, wind, got_wind)
+    )(weights, height, got_height, wind)
 
 
 def unfold_kernel(rows_ref, out_ref, lanes_ref, whole_ref, sems):
@@ -431,13 +433,10 @@
     height, wind = forecast(state, first, second, depth, bands)
     same_core = [[2 * q + core for q in range(chips)] for core in range(2)]
 
-    def to_sibling(values):
-        return lax.ppermute(pick(values, 0, values.shape[-1]), "member", sibling)
-
     height = exchange(height.reshape(chips, 2, members, cols), "member", same_core)
     height, wind = lax.optimization_barrier((height, wind))
-    wind = exchange(wind.reshape(chips, 2, members, 2 * cols), "member", same_core)
-    got_height = to_sibling(height)
+    wind = exchange(wind, "member").reshape(ensemble, 2 * cols)
+    got_height = lax.ppermute(pick(height, 0, cols), "member", sibling)
 
     keep, send = gram_of(height, got_height, obs_cell[0], obs_value[0], obs_var[0])
     half = keep + lax.ppermute(send, "member", sibling)
@@ -456,7 +455,7 @@
     far = lax.ppermute(half, ("member", "space"), beside)
     weights = transform(half + near, lax.ppermute(half, "member", sibling) + far)
 
-    analysed = mix(weights, height, got_height, wind, to_sibling(wind))
+    analysed = mix(weights, height, got_height, wind)
     back = exchange(analysed.reshape(tiles, members, fields * cols), "member").reshape(ensemble, fields * cols)
     return unfold(back, (members, fields, rows, cols)).transpose(0, 2, 1, 3)
 

time: 147 us -> 146 us (level); the launches traced: 147 us -> 144 us
  blocking collectives: 75.7 us -> 73.1 us
    ppermute x2 -> x1, starting transfers between devices: 10.8 us -> 0.32 us  [shards(): got_height = lax.ppermute(pick(height, 0, cols), 'member', sibling)]
    all_to_all x1, starting transfers between devices: 3.79 us -> 7.43 us  [exchange(): lax.all_to_all(blocks, axis, split_axis=0, concat_axis=0, tiled=True, axi...]
    ppermute x1, starting transfers between devices: 1.66 us -> 4.93 us  [shards(): near = lax.ppermute(half, 'space', [(i, i ^ 4) for i in range(bands)])]
    ppermute x1, starting transfers between devices: 0.25 us -> 3.49 us  [shards(): far = lax.ppermute(half, ('member', 'space'), beside)]
    all_to_all x2, blocking collectives: 75.7 us -> 73.1 us  [exchange(): lax.all_to_all(blocks, axis, split_axis=0, concat_axis=0, tiled=True, axi...]
    ppermute x1, waiting for transfers between devices: 2.1 us -> 0.01 us  [shards(): near = lax.ppermute(half, 'space', [(i, i ^ 4) for i in range(bands)])]
  transfers between devices with their start and end apart: 18 -> 17, of which waited for: 10 -> 10; matrix products, arithmetic and copies ran while one was open for 0% -> 0% of each run, Pallas kernels for 3% -> 1%
where the time goes in v1:
time: 146 us; the launch traced here: 144 us
  blocking collectives  73.1 us (50%)
  starting transfers between devices  35.1 us (24%)
  waiting for transfers between devices  23.6 us (16%)
  Pallas kernels  11.8 us (8%)
    all_to_all x2, blocking collectives, exchange(): lax.all_to_all(blocks, axis, split_axis=0, concat_axis=0, tiled=True, axi...  73.1 us
    ppermute x9, starting transfers between devices, others(): lax.ppermute(value, axis, [(i, i ^ unit * k) for i in range(lax.axis_size...  15.7 us
    ppermute x9, waiting for transfers between devices, others(): lax.ppermute(value, axis, [(i, i ^ unit * k) for i in range(lax.axis_size...  13.8 us
    all_to_all x1, starting transfers between devices, exchange(): lax.all_to_all(blocks, axis, split_axis=0, concat_axis=0, tiled=True, axi...  7.43 us
    ppermute x1, starting transfers between devices, shards(): near = lax.ppermute(half, 'space', [(i, i ^ 4) for i in range(bands)])  4.93 us
    ppermute x1, waiting for transfers between devices, shards(): first = lax.ppermute(first, 'space', upper)  4.68 us
    ppermute x1, starting transfers between devices, shards(): far = lax.ppermute(half, ('member', 'space'), beside)  3.49 us
    pallas_call x1, Pallas kernels, transform(): pl.pallas_call(transform_kernel, out_shape=jax.ShapeDtypeStruct((count, c...  3.35 us
  transfers between devices with their start and end apart: 17, of which 10 were waited for; matrix products, arithmetic and copies ran while one was open for 0% of the time, Pallas kernels for 1%

profile of v1, /device:TPU:1, one launch (start us, length us, event | category | flops | bytes accessed | tf_op | source)
XLA Modules:
  0.0 144.0 jit_solution(16887452129096359925)
XLA Ops:
  0.0 2.3 %edges.1 = (f32[4,136,128]{2,1,0:T(8,128)}, f32[4,136,128]{2,1,0:T(8,128)}) custom-call(f32[8,3,32,512]{3,2,1,0:T(8,128)} %bitcast.9, f32[32,512]{1,0:T(8,128)} %depth_ref.3), custom_call_target="tpu_custom_call" | custom-call | bytes 786432 | tf_op jit(solution)/shard_map/edges/pallas_call | solution.py:92
  2.3 2.1 %collective-permute-start = (f32[4,136,128]{2,1,0:T(8,128)}, f32[4,136,128]{2,1,0:T(8,128)S(1)}, u32[]{:S(2)}, u32[]{:S(2)}) collective-permute-start(f32[4,136,128]{2,1,0:T(8,128)} %get-tuple-element.15), channel_id=1, source_target_pairs={{0,1},{1,0},{2,3},{3,2},{4,5},{5,4},{6,7},{7,6},{8,9},{9,8},{10,11... | collective-permute-start | bytes 835592 | tf_op jit(solution)/shard_map/ppermute | solution.py:431
  4.4 0.7 collective-permute-start.1
  5.1 4.7 %collective-permute-done.first_ref = f32[4,136,128]{2,1,0:T(8,128)S(1)} collective-permute-done((f32[4,136,128]{2,1,0:T(8,128)}, f32[4,136,128]{2,1,0:T(8,128)S(1)}, u32[]{:S(2)}, u32[]{:S(2)}) %collective-permute-start) | collective-permute-done | bytes 278560 | tf_op jit(solution)/shard_map/ppermute | solution.py:431
  9.8 3.0 %forecast.1 = (f32[32,8,512]{2,1,0:T(8,128)S(1)}, f32[32,8,1024]{2,1,0:T(8,128)}) custom-call(f32[8,3,32,512]{3,2,1,0:T(8,128)S(1)} %bitcast.10, f32[4,136,128]{2,1,0:T(8,128)S(1)} %collective-permute-done.first_ref, f32[4,136,128]{2,1,0:T(8,128)S(1)} %collective-permute-done.1.second_ref, f32[32,512]{1,0:T(8,128)S(1)} %copy-done.1), custom_call_target="tpu_custom_call" | custom-call | flops 14155776 | bytes 3145728 | tf_op jit(solution)/shard_map/forecast/pallas_call | solution.py:207
  12.8 27.3 %all_to_all.15.state_ref.height_ref = f32[16,2,8,512]{3,2,1,0:T(8,128)S(1)} all-to-all(f32[16,2,8,512]{3,2,1,0:T(8,128)S(1)} %bitcast.14), channel_id=1, replica_groups={{0,16,32,48,64,80,96,112,128,144,160,176,192,208,224,240},{8,24,40,56,7..., dimensions={0} | all-to-all | bytes 1048576 | tf_op jit(solution)/shard_map/all_to_all | solution.py:417
  40.1 7.4 %all-to-all-start.1 = ((f32[32,8,1024]{2,1,0:T(8,128)}), f32[32,8,1024]{2,1,0:T(8,128)S(1)}, u32[]{:S(2)}, u32[]{:S(2)}) async-start(f32[32,8,1024]{2,1,0:T(8,128)} %get-tuple-element.22), calls=%async_computation.1 | async-start | bytes 2097152 | tf_op jit(solution)/shard_map/all_to_all | solution.py:417
  47.6 0.3 collective-permute-start.2
  47.9 1.3 collective-permute-done.2.got_ref.got_height_ref
  49.2 0.9 gram.1
  50.1 0.3 collective-permute-start.3
  50.4 1.0 collective-permute-done.3
  51.4 5.3 %collective-permute-start.6 = (f32[72,256]{1,0:T(8,128)S(1)}, f32[72,256]{1,0:T(8,128)S(1)}, u32[]{:S(2)}, u32[]{:S(2)}) collective-permute-start(f32[72,256]{1,0:T(8,128)S(1)} %add.36), channel_id=1, source_target_pairs={{0,3},{1,2},{2,1},{3,0},{4,7},{5,6},{6,5},{7,4},{8,11},{9,10},{10,... | collective-permute-start | bytes 221192 | tf_op jit(solution)/shard_map/ppermute | solution.py:445
  56.8 1.0 collective-permute-start.5
  57.8 2.0 %collective-permute-done.6 = f32[72,256]{1,0:T(8,128)S(1)} collective-permute-done((f32[72,256]{1,0:T(8,128)S(1)}, f32[72,256]{1,0:T(8,128)S(1)}, u32[]{:S(2)}, u32[]{:S(2)}) %collective-permute-start.6) | collective-permute-done | bytes 73760 | tf_op jit(solution)/shard_map/ppermute | solution.py:445
  59.8 1.9 %collective-permute-done.5 = f32[72,256]{1,0:T(8,128)S(1)} collective-permute-done((f32[72,256]{1,0:T(8,128)S(1)}, f32[72,256]{1,0:T(8,128)S(1)}, u32[]{:S(2)}, u32[]{:S(2)}) %collective-permute-start.5) | collective-permute-done | bytes 73760 | tf_op jit(solution)/shard_map/ppermute | solution.py:445
  61.8 2.8 %collective-permute-start.9 = (f32[72,256]{1,0:T(8,128)S(1)}, f32[72,256]{1,0:T(8,128)S(1)}, u32[]{:S(2)}, u32[]{:S(2)}) collective-permute-start(f32[72,256]{1,0:T(8,128)S(1)} %add_add_fusion.2), channel_id=1, source_target_pairs={{0,192},{8,200},{16,208},{24,216},{32,224},{40,232},{48,240},{56,2... | collective-permute-start | bytes 221192 | tf_op jit(solution)/shard_map/ppermute | solution.py:445
  64.6 0.5 collective-permute-start.8
  65.1 0.2 collective-permute-start.7
  65.3 1.4 collective-permute-done.9
  66.7 2.8 %collective-permute-done.8 = f32[72,256]{1,0:T(8,128)S(1)} collective-permute-done((f32[72,256]{1,0:T(8,128)S(1)}, f32[72,256]{1,0:T(8,128)S(1)}, u32[]{:S(2)}, u32[]{:S(2)}) %collective-permute-start.8) | collective-permute-done | bytes 73760 | tf_op jit(solution)/shard_map/ppermute | solution.py:445
  69.5 3.6 %collective-permute-start.12 = (f32[72,256]{1,0:T(8,128)S(1)}, f32[72,256]{1,0:T(8,128)S(1)}, u32[]{:S(2)}, u32[]{:S(2)}) collective-permute-start(f32[72,256]{1,0:T(8,128)S(1)} %add_add_fusion.1), channel_id=1, source_target_pairs={{0,48},{8,56},{16,32},{24,40},{32,16},{40,24},{48,0},{56,8},{64,11... | collective-permute-start | bytes 221192 | tf_op jit(solution)/shard_map/ppermute | solution.py:445
  73.1 2.3 %collective-permute-start.11 = (f32[72,256]{1,0:T(8,128)S(1)}, f32[72,256]{1,0:T(8,128)S(1)}, u32[]{:S(2)}, u32[]{:S(2)}) collective-permute-start(f32[72,256]{1,0:T(8,128)S(1)} %add_add_fusion.1), channel_id=1, source_target_pairs={{0,32},{8,40},{16,48},{24,56},{32,0},{40,8},{48,16},{56,24},{64,96... | collective-permute-start | bytes 221192 | tf_op jit(solution)/shard_map/ppermute | solution.py:445
  75.4 1.6 %collective-permute-done.12 = f32[72,256]{1,0:T(8,128)S(1)} collective-permute-done((f32[72,256]{1,0:T(8,128)S(1)}, f32[72,256]{1,0:T(8,128)S(1)}, u32[]{:S(2)}, u32[]{:S(2)}) %collective-permute-start.12) | collective-permute-done | bytes 73760 | tf_op jit(solution)/shard_map/ppermute | solution.py:445
  77.0 4.1 %collective-permute-done.11 = f32[72,256]{1,0:T(8,128)S(1)} collective-permute-done((f32[72,256]{1,0:T(8,128)S(1)}, f32[72,256]{1,0:T(8,128)S(1)}, u32[]{:S(2)}, u32[]{:S(2)}) %collective-permute-start.11) | collective-permute-done | bytes 73760 | tf_op jit(solution)/shard_map/ppermute | solution.py:445
  81.1 4.9 %collective-permute-start.13 = (f32[72,256]{1,0:T(8,128)S(1)}, f32[72,256]{1,0:T(8,128)S(1)}, u32[]{:S(2)}, u32[]{:S(2)}) collective-permute-start(f32[72,256]{1,0:T(8,128)S(1)} %add_add_fusion), channel_id=1, source_target_pairs={{0,4},{1,5},{2,6},{3,7},{4,0},{5,1},{6,2},{7,3},{8,12},{9,13},{10,... | collective-permute-start | bytes 221192 | tf_op jit(solution)/shard_map/ppermute | solution.py:454
  86.0 3.5 %collective-permute-start.15 = (f32[72,256]{1,0:T(8,128)S(1)}, f32[72,256]{1,0:T(8,128)S(1)}, u32[]{:S(2)}, u32[]{:S(2)}) collective-permute-start(f32[72,256]{1,0:T(8,128)S(1)} %add_add_fusion), channel_id=1, source_target_pairs={{0,12},{1,13},{2,14},{3,15},{4,8},{5,9},{6,10},{7,11},{8,4},{9,5},... | collective-permute-start | bytes 221192 | tf_op jit(solution)/shard_map/ppermute | solution.py:455
  89.6 2.8 %collective-permute-done.15 = f32[72,256]{1,0:T(8,128)S(1)} collective-permute-done((f32[72,256]{1,0:T(8,128)S(1)}, f32[72,256]{1,0:T(8,128)S(1)}, u32[]{:S(2)}, u32[]{:S(2)}) %collective-permute-start.15) | collective-permute-done | bytes 73760 | tf_op jit(solution)/shard_map/ppermute | solution.py:455
  92.4 3.4 %transform.1.weights_ref = f32[256,256]{1,0:T(8,128)S(1)} custom-call(f32[72,256]{1,0:T(8,128)S(1)} %add.46.keep_ref, f32[72,256]{1,0:T(8,128)S(1)} %add.47.got_ref), custom_call_target="tpu_custom_call" | custom-call | flops 2818572288 | bytes 524288 | tf_op jit(solution)/shard_map/transform/pallas_call | solution.py:341
  95.8 0.9 mix.1
  96.7 45.8 %all_to_all.16 = f32[32,8,1536]{2,1,0:T(8,128)S(1)} all-to-all(f32[32,8,1536]{2,1,0:T(8,128)S(1)} %bitcast.11), channel_id=1, replica_groups=mesh['member'=32,'space'=8] {'member'}, dimensions={0} | all-to-all | bytes 3145728 | tf_op jit(solution)/shard_map/all_to_all | solution.py:417
  142.5 1.3 unfold.1
  (27 shorter events, 0.3 us)
Async XLA Ops:
  0.0 9.8 %copy-start.1 = (f32[32,512]{1,0:T(8,128)S(1)}, f32[32,512]{1,0:T(8,128)}, u32[]{:S(2)}) copy-start(f32[32,512]{1,0:T(8,128)} %depth_ref.3) | copy-start | bytes 196612
  0.0 9.8 %copy-start = (f32[8,32,3,512]{3,1,2,0:T(8,128)S(1)}, f32[8,32,3,512]{3,1,2,0:T(8,128)}, u32[]{:S(2)}) copy-start(f32[8,32,3,512]{3,1,2,0:T(8,128)} %param.5) | copy-start | bytes 4718596
  2.3 7.5 %collective-permute-start = (f32[4,136,128]{2,1,0:T(8,128)}, f32[4,136,128]{2,1,0:T(8,128)S(1)}, u32[]{:S(2)}, u32[]{:S(2)}) collective-permute-start(f32[4,136,128]{2,1,0:T(8,128)} %get-tuple-element.15), channel_id=1, source_target_pairs={{0,1},{1,0},{2,3},{3,2},{4,5},{5,4},{6,7},{7,6},{8,9},{9,8},{10,11... | collective-permute-start | bytes 835592 | tf_op jit(solution)/shard_map/ppermute | solution.py:431
  4.4 5.4 %collective-permute-start.1 = (f32[4,136,128]{2,1,0:T(8,128)}, f32[4,136,128]{2,1,0:T(8,128)S(1)}, u32[]{:S(2)}, u32[]{:S(2)}) collective-permute-start(f32[4,136,128]{2,1,0:T(8,128)} %get-tuple-element.16), channel_id=1, source_target_pairs={{1,2},{2,1},{3,4},{4,3},{5,6},{6,5},{9,10},{10,9},{11,12},{12,11},... | collective-permute-start | bytes 835592 | tf_op jit(solution)/shard_map/ppermute | solution.py:432
  40.1 9.1 %copy-start.2 = (s32[1,1,32]{2,1,0:T(1,128)S(1)}, s32[1,1,32]{2,1,0:T(1,128)}, u32[]{:S(2)}) copy-start(s32[1,1,32]{2,1,0:T(1,128)} %param.7) | copy-start | bytes 388
  40.1 9.1 %copy-start.3 = (f32[1,1,32]{2,1,0:T(1,128)S(1)}, f32[1,1,32]{2,1,0:T(1,128)}, u32[]{:S(2)}) copy-start(f32[1,1,32]{2,1,0:T(1,128)} %param.8) | copy-start | bytes 388
  40.1 9.1 %copy-start.4 = (f32[1,1,32]{2,1,0:T(1,128)S(1)}, f32[1,1,32]{2,1,0:T(1,128)}, u32[]{:S(2)}) copy-start(f32[1,1,32]{2,1,0:T(1,128)} %param.9) | copy-start | bytes 388
  40.1 41.0 %all-to-all-start.1 = ((f32[32,8,1024]{2,1,0:T(8,128)}), f32[32,8,1024]{2,1,0:T(8,128)S(1)}, u32[]{:S(2)}, u32[]{:S(2)}) async-start(f32[32,8,1024]{2,1,0:T(8,128)} %get-tuple-element.22), calls=%async_computation.1 | async-start | bytes 2097152 | tf_op jit(solution)/shard_map/all_to_all | solution.py:417
  47.6 1.6 %collective-permute-start.2 = (f32[16,8,512]{2,1,0:T(8,128)S(1)}, f32[16,8,512]{2,1,0:T(8,128)S(1)}, u32[]{:S(2)}, u32[]{:S(2)}) collective-permute-start(f32[16,8,512]{2,1,0:T(8,128)S(1)} %pick.1), channel_id=1, source_target_pairs={{0,8},{8,0},{16,24},{24,16},{32,40},{40,32},{48,56},{56,48},{64,72... | collective-permute-start | bytes 786440 | tf_op jit(solution)/shard_map/ppermute | solution.py:439
  50.1 1.3 collective-permute-start.3
  51.4 8.4 %collective-permute-start.6 = (f32[72,256]{1,0:T(8,128)S(1)}, f32[72,256]{1,0:T(8,128)S(1)}, u32[]{:S(2)}, u32[]{:S(2)}) collective-permute-start(f32[72,256]{1,0:T(8,128)S(1)} %add.36), channel_id=1, source_target_pairs={{0,3},{1,2},{2,1},{3,0},{4,7},{5,6},{6,5},{7,4},{8,11},{9,10},{10,... | collective-permute-start | bytes 221192 | tf_op jit(solution)/shard_map/ppermute | solution.py:445
  56.8 5.0 %collective-permute-start.5 = (f32[72,256]{1,0:T(8,128)S(1)}, f32[72,256]{1,0:T(8,128)S(1)}, u32[]{:S(2)}, u32[]{:S(2)}) collective-permute-start(f32[72,256]{1,0:T(8,128)S(1)} %add.36), channel_id=1, source_target_pairs={{0,2},{1,3},{2,0},{3,1},{4,6},{5,7},{6,4},{7,5},{8,10},{9,11},{10,... | collective-permute-start | bytes 221192 | tf_op jit(solution)/shard_map/ppermute | solution.py:445
  57.8 4.0 %collective-permute-start.4 = (f32[72,256]{1,0:T(8,128)S(1)}, f32[72,256]{1,0:T(8,128)S(1)}, u32[]{:S(2)}, u32[]{:S(2)}) collective-permute-start(f32[72,256]{1,0:T(8,128)S(1)} %add.36), channel_id=1, source_target_pairs={{0,1},{1,0},{2,3},{3,2},{4,5},{5,4},{6,7},{7,6},{8,9},{9,8},{10,11... | collective-permute-start | bytes 221192 | tf_op jit(solution)/shard_map/ppermute | solution.py:445
  61.8 5.0 %collective-permute-start.9 = (f32[72,256]{1,0:T(8,128)S(1)}, f32[72,256]{1,0:T(8,128)S(1)}, u32[]{:S(2)}, u32[]{:S(2)}) collective-permute-start(f32[72,256]{1,0:T(8,128)S(1)} %add_add_fusion.2), channel_id=1, source_target_pairs={{0,192},{8,200},{16,208},{24,216},{32,224},{40,232},{48,240},{56,2... | collective-permute-start | bytes 221192 | tf_op jit(solution)/shard_map/ppermute | solution.py:445
  64.6 4.9 %collective-permute-start.8 = (f32[72,256]{1,0:T(8,128)S(1)}, f32[72,256]{1,0:T(8,128)S(1)}, u32[]{:S(2)}, u32[]{:S(2)}) collective-permute-start(f32[72,256]{1,0:T(8,128)S(1)} %add_add_fusion.2), channel_id=1, source_target_pairs={{0,128},{8,136},{16,144},{24,152},{32,160},{40,168},{48,176},{56,1... | collective-permute-start | bytes 221192 | tf_op jit(solution)/shard_map/ppermute | solution.py:445
  65.1 4.4 %collective-permute-start.7 = (f32[72,256]{1,0:T(8,128)S(1)}, f32[72,256]{1,0:T(8,128)S(1)}, u32[]{:S(2)}, u32[]{:S(2)}) collective-permute-start(f32[72,256]{1,0:T(8,128)S(1)} %add_add_fusion.2), channel_id=1, source_target_pairs={{0,64},{8,72},{16,80},{24,88},{32,96},{40,104},{48,112},{56,120},{... | collective-permute-start | bytes 221192 | tf_op jit(solution)/shard_map/ppermute | solution.py:445
  69.5 7.4 %collective-permute-start.12 = (f32[72,256]{1,0:T(8,128)S(1)}, f32[72,256]{1,0:T(8,128)S(1)}, u32[]{:S(2)}, u32[]{:S(2)}) collective-permute-start(f32[72,256]{1,0:T(8,128)S(1)} %add_add_fusion.1), channel_id=1, source_target_pairs={{0,48},{8,56},{16,32},{24,40},{32,16},{40,24},{48,0},{56,8},{64,11... | collective-permute-start | bytes 221192 | tf_op jit(solution)/shard_map/ppermute | solution.py:445
  73.1 7.9 %collective-permute-start.11 = (f32[72,256]{1,0:T(8,128)S(1)}, f32[72,256]{1,0:T(8,128)S(1)}, u32[]{:S(2)}, u32[]{:S(2)}) collective-permute-start(f32[72,256]{1,0:T(8,128)S(1)} %add_add_fusion.1), channel_id=1, source_target_pairs={{0,32},{8,40},{16,48},{24,56},{32,0},{40,8},{48,16},{56,24},{64,96... | collective-permute-start | bytes 221192 | tf_op jit(solution)/shard_map/ppermute | solution.py:445
  75.4 5.7 %collective-permute-start.10 = (f32[72,256]{1,0:T(8,128)S(1)}, f32[72,256]{1,0:T(8,128)S(1)}, u32[]{:S(2)}, u32[]{:S(2)}) collective-permute-start(f32[72,256]{1,0:T(8,128)S(1)} %add_add_fusion.1), channel_id=1, source_target_pairs={{0,16},{8,24},{16,0},{24,8},{32,48},{40,56},{48,32},{56,40},{64,80... | collective-permute-start | bytes 221192 | tf_op jit(solution)/shard_map/ppermute | solution.py:445
  81.1 8.5 %collective-permute-start.13 = (f32[72,256]{1,0:T(8,128)S(1)}, f32[72,256]{1,0:T(8,128)S(1)}, u32[]{:S(2)}, u32[]{:S(2)}) collective-permute-start(f32[72,256]{1,0:T(8,128)S(1)} %add_add_fusion), channel_id=1, source_target_pairs={{0,4},{1,5},{2,6},{3,7},{4,0},{5,1},{6,2},{7,3},{8,12},{9,13},{10,... | collective-permute-start | bytes 221192 | tf_op jit(solution)/shard_map/ppermute | solution.py:454
  86.0 6.4 %collective-permute-start.15 = (f32[72,256]{1,0:T(8,128)S(1)}, f32[72,256]{1,0:T(8,128)S(1)}, u32[]{:S(2)}, u32[]{:S(2)}) collective-permute-start(f32[72,256]{1,0:T(8,128)S(1)} %add_add_fusion), channel_id=1, source_target_pairs={{0,12},{1,13},{2,14},{3,15},{4,8},{5,9},{6,10},{7,11},{8,4},{9,5},... | collective-permute-start | bytes 221192 | tf_op jit(solution)/shard_map/ppermute | solution.py:455
  89.5 2.9 %collective-permute-start.14 = (f32[72,256]{1,0:T(8,128)S(1)}, f32[72,256]{1,0:T(8,128)S(1)}, u32[]{:S(2)}, u32[]{:S(2)}) collective-permute-start(f32[72,256]{1,0:T(8,128)S(1)} %add_add_fusion), channel_id=1, source_target_pairs={{0,8},{8,0},{16,24},{24,16},{32,40},{40,32},{48,56},{56,48},{64,72... | collective-permute-start | bytes 221192 | tf_op jit(solution)/shard_map/ppermute | solution.py:456
